TPU v7x, 32 devices: a whole 2x2x4 slice. The times are simulated.
32 devices in a mesh: groups: 2 (over y), adapter: 16 (over z, x, core).
Axes of the slice: x: 2, y: 2, z: 4, core: 2. Of those that a mesh axis runs over, the one named last changes fastest.
Arguments:
- tokens: bfloat16 [1024, 8, 3200], P(('groups', 'adapter')), parts along dimension 0, may hold values from -40 to 40
- request_block_adapter: int32 [1024], P(('groups', 'adapter')), parts along dimension 0, may hold values from 0 to 127, as said below
- request_block_rows: int32 [1024], P(('groups', 'adapter')), parts along dimension 0, may hold values from 1 to 8
- adapter_down_weight: bfloat16 [128, 3200, 64], P('adapter'), may hold values from -0.109375 to 0.109375
- adapter_up_weight: bfloat16 [128, 64, 3200], P('adapter'), may hold values from -0.75 to 0.75
Outputs:
- mixed: bfloat16 [1024, 8, 3200], P(('groups', 'adapter')), parts along dimension 0
There are 2 independent parts, one for each index of `groups`. A program takes and returns all parts, laid end to end along the dimension named above; an argument that names none is the same for every part. Nothing has to cross between parts.
Inputs may be any that keep to these rules, and one draw needn't show every extreme that they name: `request_block_adapter`: adapter a is held by the device of index a // 8. The 32 blocks of one device go to at most 8 blocks for each holding device; in every draw some devices receive exactly 8 blocks from every device.
All inputs are finite; a program needn't handle non-finite values.
Results may differ from a plain program's by a relative error of at most 0.0031.
Values may be sent and summed in bfloat16 or wider, within the bound.
No kernel may reach another device: no remote copies, remote signals or barrier semaphores. Data moves between devices by JAX's collectives and lax.ppermute only.
A program may use at most 64 MiB of HBM per device.

v0:
```python
import jax
import jax.numpy as jnp
from jax import lax
from jax.sharding import PartitionSpec as P


def normalise(tokens):
    values = tokens.astype(jnp.float32)
    mean_sq = jnp.mean(values * values, axis=-1, keepdims=True)
    return (values, (values * lax.rsqrt(mean_sq + 1e-06)).astype(jnp.bfloat16))


def resident_update(hidden_state, block_labels, adapter_down_weight, adapter_up_weight):
    feature_width = hidden_state.shape[-1]
    leading = hidden_state.shape[:-1]
    resident_rows, unused_value, inner_rank = adapter_down_weight.shape
    flattened_tokens = hidden_state.reshape(-1, feature_width)
    down_matrix = jnp.einsum(
        "tq,iqg->tig", flattened_tokens, adapter_down_weight, preferred_element_type=jnp.float32
    )
    down_matrix = down_matrix.astype(jnp.bfloat16).reshape(
        flattened_tokens.shape[0], resident_rows * inner_rank
    )
    column_owner = jnp.arange(resident_rows * inner_rank, dtype=jnp.int32) // inner_rank
    picked = block_labels.reshape(-1, 1) == column_owner[None, :]
    down_matrix = jnp.where(picked, down_matrix, jnp.zeros_like(down_matrix))
    lowrank_update = jnp.dot(
        down_matrix,
        adapter_up_weight.reshape(resident_rows * inner_rank, feature_width),
        preferred_element_type=jnp.float32,
    )
    return lowrank_update.astype(jnp.bfloat16).reshape(leading + (feature_width,))


def per_device(
    tokens, request_block_adapter, request_block_rows, adapter_down_weight, adapter_up_weight
):
    blocks, rows, feature_width = tokens.shape
    devices = lax.axis_size("adapter")
    resident_rows = adapter_down_weight.shape[0]
    slots = max(1, 4 * blocks // devices)
    values, normed = normalise(tokens)
    owner = request_block_adapter // resident_rows
    within = request_block_adapter - owner * resident_rows
    serial = jnp.arange(blocks, dtype=jnp.int32)
    earlier = (owner[:, None] == owner[None, :]) & (serial[None, :] < serial[:, None])
    position = owner * slots + jnp.sum(earlier, axis=1)
    outgoing = (
        jnp.zeros((devices * slots, rows, feature_width), jnp.bfloat16).at[position].set(normed)
    )
    outgoing = outgoing.reshape(devices, slots, rows, feature_width)
    block_labels = jnp.full((devices * slots,), -1, jnp.int32).at[position].set(within)
    block_labels = jnp.broadcast_to(block_labels[:, None], (devices * slots, rows)).reshape(
        devices, slots, rows
    )
    arriving_rows, row_markers = (
        lax.all_to_all(outgoing, "adapter", split_axis=0, concat_axis=0, tiled=True),
        lax.all_to_all(block_labels, "adapter", split_axis=0, concat_axis=0, tiled=True),
    )
    lowrank_update = resident_update(
        arriving_rows, row_markers, adapter_down_weight, adapter_up_weight
    )
    returned = lax.all_to_all(lowrank_update, "adapter", split_axis=0, concat_axis=0, tiled=True)
    mine = returned.reshape(devices * slots, rows, feature_width)[position]
    live = jnp.arange(rows, dtype=jnp.int32)[None, :] < request_block_rows[:, None]
    mixed = values + jnp.where(live[:, :, None], mine.astype(jnp.float32), jnp.float32(0.0))
    return mixed.astype(jnp.bfloat16)


def solution(mesh):
    placed = (
        P(("groups", "adapter"), None, None),
        P(("groups", "adapter")),
        P(("groups", "adapter")),
        P("adapter", None, None),
        P("adapter", None, None),
    )
    return jax.shard_map(
        per_device,
        mesh=mesh,
        in_specs=placed,
        out_specs=P(("groups", "adapter"), None, None),
        check_vma=False,
    )
```

profile of v0, /device:TPU:11, one launch (start us, length us, event | category | flops | bytes accessed | tf_op | source)
XLA Modules:
  0.0 341.3 jit_solution(599621556772558339)
XLA Ops:
  0.0 0.0 copy-start
  0.0 0.8 multiply_subtract_fusion
  0.8 0.2 convert_reduce_fusion
  1.0 0.7 scatter_custom_fusion
  1.7 0.1 broadcast_in_dim.46
  1.8 0.7 broadcast_in_dim.47
  2.5 6.6 %all-to-all-start = ((s32[16,8,8]{2,1,0:T(8,128)}), s32[16,8,8]{2,1,0:T(8,128)S(1)}, u32[]{:S(2)}, u32[]{:S(2)}) async-start(s32[16,8,8]{2,1,0:T(8,128)} %broadcast_in_dim.47), calls=%async_computation | async-start | bytes 131072 | tf_op jit(solution)/shard_map/all_to_all | solution.py:58
  9.0 1.8 fusion
  10.9 3.0 fusion.1
  13.9 3.1 broadcast_in_dim.48
  17.0 5.9 %scatter_fusion = bf16[128,8,3200]{2,1,0:T(8,128)(2,1)} fusion(bf16[128,8,3200]{2,1,0:T(8,128)(2,1)} %broadcast_in_dim.48, s32[32]{0:T(128)S(1)} %compare_select_fusion.2, bf16[32,8,3200]{2,1,0:T(8,128)(2,1)} %fusion.1), kind=kCustom, calls=%fused_computation.2 | custom fusion | bytes 4915328 | tf_op jit(solution)/shard_map/scatter | solution.py:49
  22.9 0.0 all-to-all-done
  22.9 6.0 %all-to-all-start.1 = ((bf16[16,8,8,3200]{3,2,1,0:T(8,128)(2,1)}), bf16[16,8,8,3200]{3,2,1,0:T(8,128)(2,1)}, u32[]{:S(2)}, u32[]{:S(2)}) async-start(bf16[16,8,8,3200]{3,2,1,0:T(8,128)(2,1)} %bitcast.13), calls=%async_computation.1 | async-start | bytes 13107200 | tf_op jit(solution)/shard_map/all_to_all | solution.py:57
  28.9 0.1 eq.32
  29.0 142.9 %all-to-all-done.1 = bf16[16,8,8,3200]{3,2,1,0:T(8,128)(2,1)} async-done(((bf16[16,8,8,3200]{3,2,1,0:T(8,128)(2,1)}), bf16[16,8,8,3200]{3,2,1,0:T(8,128)(2,1)}, u32[]{:S(2)}, u32[]{:S(2)}) %all-to-all-start.1) | async-done | bytes 6553632 | tf_op jit(solution)/shard_map/all_to_all | solution.py:57
  171.9 6.9 %fusion.12 = f32[1024,512]{0,1:S(1)} fusion(bf16[1024,3200]{1,0:T(8,128)(2,1)} %bitcast.1, bf16[3200,512]{0,1:T(8,128)(2,1)} %bitcast.15), kind=kOutput, calls=%fused_computation.35 | convolution fusion | flops 3355443200 | bytes 11927552
  178.8 0.0 copy-done
  178.8 5.9 %bitcast_convert_fusion = bf16[1024,3200]{1,0:T(8,128)(2,1)} fusion(bf16[8,64,3200]{2,1,0:T(8,128)(2,1)S(1)} %copy-done, f32[1024,8,64]{0,2,1:T(8,128)S(1)} %bitcast.16, s32[8,64]{1,0:T(8,128)S(1)} %add_select_fusion, s32[1024]{0:T(1024)S(1)} %eq.32), kind=kOutput, calls=%fused_computation.3 | convolution fusion | flops 3360292864 | bytes 11933696 | tf_op jit(solution)/shard_map/dot_general | solution.py:27
  184.7 5.0 %all-to-all-start.2 = ((bf16[16,8,8,3200]{3,2,1,0:T(8,128)(2,1)}), bf16[16,8,8,3200]{3,2,1,0:T(8,128)(2,1)}, u32[]{:S(2)}, u32[]{:S(2)}) async-start(bf16[16,8,8,3200]{3,2,1,0:T(8,128)(2,1)} %bitcast.14), calls=%async_computation.2 | async-start | bytes 13107200 | tf_op jit(solution)/shard_map/all_to_all | solution.py:63
  189.7 0.0 copy-done.1
  189.7 0.1 iota_compare_fusion.1
  189.8 142.9 %all-to-all-done.2 = bf16[16,8,8,3200]{3,2,1,0:T(8,128)(2,1)} async-done(((bf16[16,8,8,3200]{3,2,1,0:T(8,128)(2,1)}), bf16[16,8,8,3200]{3,2,1,0:T(8,128)(2,1)}, u32[]{:S(2)}, u32[]{:S(2)}) %all-to-all-start.2) | async-done | bytes 6553632 | tf_op jit(solution)/shard_map/all_to_all | solution.py:63
  332.8 4.7 %gather_fusion = bf16[32,8,3200]{2,1,0:T(8,128)(2,1)} fusion(bf16[128,8,3200]{2,1,0:T(8,128)(2,1)} %bitcast.7, s32[1024]{0:T(1024)S(1)} %pad_clamp_fusion), kind=kCustom, calls=%fused_computation | custom fusion | bytes 3276928 | tf_op jit(solution)/shard_map/gather | solution.py:64
  337.5 3.8 %fusion.2 = bf16[32,8,3200]{2,1,0:T(8,128)(2,1)} fusion(bf16[32,8,3200]{2,1,0:T(8,128)(2,1)} %param.5, bf16[32,8,3200]{2,1,0:T(8,128)(2,1)} %gather_fusion, pred[32,8]{1,0:T(8,128)(4,1)S(1)} %iota_compare_fusion.1), kind=kLoop, calls=%fused_computation.9 | loop fusion | flops 4096000 | bytes 4915456 | tf_op jit(solution)/shard_map/convert_element_type | solution.py:67
  (5 shorter events, 0.0 us)
Async XLA Ops:
  0.0 178.8 %copy-start = (bf16[8,64,3200]{2,1,0:T(8,128)(2,1)S(1)}, bf16[8,64,3200]{2,1,0:T(8,128)(2,1)}, u32[]{:S(2)}) copy-start(bf16[8,64,3200]{2,1,0:T(8,128)(2,1)} %param.9) | copy-start | bytes 9830404
  2.5 20.4 %all-to-all-start = ((s32[16,8,8]{2,1,0:T(8,128)}), s32[16,8,8]{2,1,0:T(8,128)S(1)}, u32[]{:S(2)}, u32[]{:S(2)}) async-start(s32[16,8,8]{2,1,0:T(8,128)} %broadcast_in_dim.47), calls=%async_computation | async-start | bytes 131072 | tf_op jit(solution)/shard_map/all_to_all | solution.py:58
  22.9 149.0 %all-to-all-start.1 = ((bf16[16,8,8,3200]{3,2,1,0:T(8,128)(2,1)}), bf16[16,8,8,3200]{3,2,1,0:T(8,128)(2,1)}, u32[]{:S(2)}, u32[]{:S(2)}) async-start(bf16[16,8,8,3200]{3,2,1,0:T(8,128)(2,1)} %bitcast.13), calls=%async_computation.1 | async-start | bytes 13107200 | tf_op jit(solution)/shard_map/all_to_all | solution.py:57
  184.7 5.1 %copy-start.1 = (s32[32]{0:T(128)S(1)}, s32[32]{0:T(128)}, u32[]{:S(2)}) copy-start(s32[32]{0:T(128)} %param.7) | copy-start | bytes 388
  184.7 148.1 %all-to-all-start.2 = ((bf16[16,8,8,3200]{3,2,1,0:T(8,128)(2,1)}), bf16[16,8,8,3200]{3,2,1,0:T(8,128)(2,1)}, u32[]{:S(2)}, u32[]{:S(2)}) async-start(bf16[16,8,8,3200]{3,2,1,0:T(8,128)(2,1)} %bitcast.14), calls=%async_computation.2 | async-start | bytes 13107200 | tf_op jit(solution)/shard_map/all_to_all | solution.py:63
where the time goes:
time: 342 us; the launch traced here: 341 us
  waiting for transfers between devices  286 us (84%)
  starting transfers between devices  17.6 us (5%)
  local copies, waits for them, and re-layouts  15.3 us (4%)
  matrix products  12.7 us (4%)
  other arithmetic  9.71 us (3%)
    all_to_all x1, waiting for transfers between devices, per_device(): lax.all_to_all(lowrank_update, 'adapter', split_axis=0, concat_axis=0, ti...  143 us
    all_to_all x1, waiting for transfers between devices, per_device(): lax.all_to_all(outgoing, 'adapter', split_axis=0, concat_axis=0, tiled=True)  143 us
    unnamed x1, matrix products  6.85 us
  transfers between devices with their start and end apart: 3, of which 2 were waited for; matrix products, arithmetic and copies ran while one was open for 4% of the time, Pallas kernels for 0%

commit v1 on v0

--- a/solution.py
+++ b/solution.py
@@ -1,7 +1,17 @@
+import functools
+
 import jax
 import jax.numpy as jnp
 from jax import lax
+from jax.experimental import pallas as pl
+from jax.experimental.pallas import tpu as pltpu
 from jax.sharding import PartitionSpec as P
+
+LANES = 128
+HALF = 64
+EIGHT = 8
+VMEM = pl.BlockSpec(memory_space=pltpu.VMEM)
+SMEM = pl.BlockSpec(memory_space=pltpu.SMEM)
 
 
 def normalise(tokens):
@@ -32,7 +42,7 @@
     return lowrank_update.astype(jnp.bfloat16).reshape(leading + (feature_width,))
 
 
-def per_device(
+def rows_to_holders(
     tokens, request_block_adapter, request_block_rows, adapter_down_weight, adapter_up_weight
 ):
     blocks, rows, feature_width = tokens.shape
@@ -67,6 +77,378 @@
     return mixed.astype(jnp.bfloat16)
 
 
+def lanes_of(rows):
+    return lax.broadcasted_iota(jnp.int32, (rows, LANES), 1)
+
+
+def pack_all(read, out_ref, devices, total):
+    half, part = total // 2, total // devices
+    low = lanes_of(half) < HALF
+    for j in range(devices):
+        out_ref[j, 0:total, :] = read(0, total, j).astype(jnp.bfloat16)
+    for i in range(devices // 2):
+        upper = read(0, half, devices + i).astype(jnp.float32)
+        lower = read(half, half, devices + i).astype(jnp.float32)
+        even = jnp.where(low, upper, pltpu.roll(lower, HALF, 1))
+        odd = jnp.where(low, pltpu.roll(upper, HALF, 1), lower)
+        out_ref[2 * i, total : total + half, :] = even.astype(jnp.bfloat16)
+        out_ref[2 * i + 1, total : total + half, :] = odd.astype(jnp.bfloat16)
+    last = devices + devices // 2
+    group = lanes_of(part) // EIGHT
+    pieces = [read(m * part, part, last).astype(jnp.float32) for m in range(devices)]
+    for j in range(devices):
+        merged = pieces[j]
+        for m in range(devices):
+            if m != j:
+                shifted = pltpu.roll(pieces[m], (EIGHT * (m - j)) % LANES, 1)
+                merged = jnp.where(group == m, shifted, merged)
+        out_ref[j, total + half : total + half + part, :] = merged.astype(jnp.bfloat16)
+
+
+def unpack_second(share, devices, total):
+    half, part = total // 2, total // devices
+    first = share[total : total + half, :].astype(jnp.float32)
+    rest = share[total + half : total + half + part, :].astype(jnp.float32)
+    halves = jnp.concatenate([first, pltpu.roll(first, HALF, 1)], axis=0)
+    eights = jnp.concatenate(
+        [pltpu.roll(rest, (HALF - EIGHT * m) % LANES, 1) for m in range(devices)], axis=0
+    )
+    return jnp.where(lanes_of(total) < HALF, halves, eights)
+
+
+def weight_pack_kernel(devices, total, which_ref, weight_ref, out_ref):
+    start = pl.multiple_of(which_ref[0] * total, total)
+
+    def read(row, count, tile):
+        return weight_ref[pl.ds(start + row, count), tile * LANES : (tile + 1) * LANES]
+
+    pack_all(read, out_ref, devices, total)
+
+
+def token_pack_kernel(devices, total, position_ref, tokens_ref, out_ref, sorted_ref):
+    blocks, rows, width = tokens_ref.shape
+
+    def one(b, carry):
+        values = tokens_ref[b].astype(jnp.float32)
+        mean_sq = jnp.mean(values * values, axis=-1, keepdims=True)
+        start = pl.multiple_of(position_ref[b] * rows, rows)
+        sorted_ref[pl.ds(start, rows), :] = values * lax.rsqrt(mean_sq + 1e-06)
+        return carry
+
+    lax.fori_loop(0, blocks, one, 0, unroll=4)
+
+    def read(row, count, tile):
+        return sorted_ref[row : row + count, tile * LANES : (tile + 1) * LANES]
+
+    pack_all(read, out_ref, devices, total)
+
+
+def fill_labels(devices, blocks, rows, labels_ref, label_rows_ref):
+    def one(b, carry):
+        for s in range(devices):
+            start = pl.multiple_of(b * rows, rows)
+            label_rows_ref[s, pl.ds(start, rows), :] = jnp.full(
+                (rows, LANES), labels_ref[s * blocks + b], jnp.int32
+            )
+        return carry
+
+    lax.fori_loop(0, blocks, one, 0)
+    total = blocks * rows
+    spare = label_rows_ref.shape[1] - total
+    for s in range(devices):
+        label_rows_ref[s, total : total + spare, :] = jnp.full((spare, LANES), -1, jnp.int32)
+
+
+def down_kernel(
+    devices,
+    blocks,
+    rows,
+    window,
+    resident,
+    labels_ref,
+    starts_ref,
+    group_ref,
+    rows_ref,
+    own_ref,
+    twin_ref,
+    out_ref,
+    spread_ref,
+    sum_ref,
+    label_rows_ref,
+):
+    total = blocks * rows
+    weight_rows = resident // 2 * HALF
+    fill_labels(devices, blocks, rows, labels_ref, label_rows_ref)
+    inside = lanes_of(total) < HALF + EIGHT
+
+    def spread(s, carry):
+        spread_ref[s, 0:total, 0:LANES] = rows_ref[s, 0:total, :].astype(jnp.float32)
+        second = unpack_second(rows_ref.at[s], devices, total)
+        spread_ref[s, 0:total, LANES:] = jnp.where(inside, second, 0.0)
+        spread_ref[s, total : total + window, :] = jnp.zeros((window, 2 * LANES), jnp.float32)
+        return carry
+
+    lax.fori_loop(0, devices, spread, 0)
+    group = group_ref[0]
+    own_at = group * (resident // 2)
+    twin_at = (1 - group) * (resident // 2)
+    upper = (lanes_of(window) >= HALF).astype(jnp.int32)
+
+    def weight_of(ref, h):
+        second = unpack_second(ref.at[h], devices, weight_rows).astype(jnp.bfloat16)
+        return jnp.concatenate([ref[h, 0:weight_rows, :], second], axis=1)
+
+    def holder(h, carry):
+        own = weight_of(own_ref, h)
+        twin = weight_of(twin_ref, h)
+        for s in range(devices):
+            start = pl.multiple_of(starts_ref[s * devices + h] * rows, rows)
+            part = spread_ref[s, pl.ds(start, window), :].astype(jnp.bfloat16)
+            label = label_rows_ref[s, pl.ds(start, window), :] - h * resident - upper
+            dims = (((1,), (1,)), ((), ()))
+            mine = lax.dot_general(part, own, dims, preferred_element_type=jnp.float32)
+            other = lax.dot_general(part, twin, dims, preferred_element_type=jnp.float32)
+            picked = jnp.zeros((window, LANES), jnp.float32)
+            for t in range(resident // 4):
+                columns = slice(t * LANES, (t + 1) * LANES)
+                picked = jnp.where(label == own_at + 2 * t, mine[:, columns], picked)
+                picked = jnp.where(label == twin_at + 2 * t, other[:, columns], picked)
+            sum_ref[s, pl.ds(start, window), :] = picked + pltpu.roll(picked, HALF, 1)
+        return carry
+
+    lax.fori_loop(0, devices, holder, 0)
+    low = lanes_of(total // 2) < HALF
+
+    def leave(s, carry):
+        out_ref[s] = jnp.where(
+            low, sum_ref[s, 0 : total // 2, :], sum_ref[s, total // 2 : total, :]
+        ).astype(out_ref.dtype)
+        return carry
+
+    lax.fori_loop(0, devices, leave, 0)
+
+
+def up_kernel(
+    devices,
+    blocks,
+    rows,
+    window,
+    resident,
+    labels_ref,
+    starts_ref,
+    group_ref,
+    down_ref,
+    own_ref,
+    twin_ref,
+    out_ref,
+    twice_ref,
+    delta_ref,
+    label_rows_ref,
+):
+    total = blocks * rows
+    half, share = total // 2, total // devices
+    weight_rows = resident // 2 * HALF
+    fill_labels(devices, blocks, rows, labels_ref, label_rows_ref)
+    low = lanes_of(half) < HALF
+
+    def spread(s, carry):
+        packed = down_ref[s].astype(jnp.bfloat16).astype(jnp.float32)
+        turned = pltpu.roll(packed, HALF, 1)
+        twice_ref[s, 0:half, :] = jnp.where(low, packed, turned)
+        twice_ref[s, half:total, :] = jnp.where(low, turned, packed)
+        twice_ref[s, total : total + window, :] = jnp.zeros((window, LANES), jnp.float32)
+        return carry
+
+    lax.fori_loop(0, devices, spread, 0)
+    group = group_ref[0]
+    own_at = group * (resident // 2)
+    twin_at = (1 - group) * (resident // 2)
+    upper = (lanes_of(window) >= HALF).astype(jnp.int32)
+
+    def weight_of(ref, h):
+        second = unpack_second(ref.at[h], devices, weight_rows).astype(jnp.bfloat16)
+        return jnp.concatenate([ref[h, 0:weight_rows, :], second], axis=1)
+
+    def holder(h, carry):
+        own = weight_of(own_ref, h)
+        twin = weight_of(twin_ref, h)
+        for s in range(devices):
+            start = pl.multiple_of(starts_ref[s * devices + h] * rows, rows)
+            part = twice_ref[s, pl.ds(start, window), :]
+            label = label_rows_ref[s, pl.ds(start, window), :] - h * resident - upper
+            sides = []
+            for at in (own_at, twin_at):
+                placed = [
+                    jnp.where(label == at + 2 * t, part, 0.0) for t in range(resident // 4)
+                ]
+                sides.append(jnp.concatenate(placed, axis=1).astype(jnp.bfloat16))
+            delta_ref[s, pl.ds(start, window), :] = jnp.dot(
+                sides[0], own, preferred_element_type=jnp.float32
+            ) + jnp.dot(sides[1], twin, preferred_element_type=jnp.float32)
+        return carry
+
+    lax.fori_loop(0, devices, holder, 0)
+    eighth = lanes_of(share) // EIGHT
+
+    def leave(s, carry):
+        out_ref[s, 0:total, :] = delta_ref[s, 0:total, 0:LANES].astype(jnp.bfloat16)
+        second = delta_ref[s, 0:total, LANES:]
+        halves = jnp.where(low, second[0:half], pltpu.roll(second[half:total], HALF, 1))
+        out_ref[s, total : total + half, :] = halves.astype(jnp.bfloat16)
+        merged = jnp.zeros((share, LANES), jnp.float32)
+        for m in range(devices):
+            piece = second[m * share : (m + 1) * share]
+            shifted = pltpu.roll(piece, (EIGHT * m - HALF) % LANES, 1)
+            merged = jnp.where(eighth == m, shifted, merged)
+        out_ref[s, total + half : total + half + share, :] = merged.astype(jnp.bfloat16)
+        return carry
+
+    lax.fori_loop(0, devices, leave, 0)
+
+
+def mix_kernel(devices, position_ref, used_ref, tokens_ref, returned_ref, out_ref, delta_ref):
+    blocks, rows, width = tokens_ref.shape
+    total = blocks * rows
+    half, share = total // 2, total // devices
+    low = lanes_of(half) < HALF
+    for j in range(devices):
+        delta_ref[:, j * LANES : (j + 1) * LANES] = returned_ref[j, 0:total, :].astype(jnp.float32)
+    for i in range(devices // 2):
+        even = returned_ref[2 * i, total : total + half, :].astype(jnp.float32)
+        odd = returned_ref[2 * i + 1, total : total + half, :].astype(jnp.float32)
+        columns = slice((devices + i) * LANES, (devices + i + 1) * LANES)
+        delta_ref[0:half, columns] = jnp.where(low, even, pltpu.roll(odd, HALF, 1))
+        delta_ref[half:total, columns] = jnp.where(low, pltpu.roll(even, HALF, 1), odd)
+    last = devices + devices // 2
+    eighth = lanes_of(share) // EIGHT
+    pieces = [
+        returned_ref[j, total + half : total + half + share, :].astype(jnp.float32)
+        for j in range(devices)
+    ]
+    for m in range(devices):
+        merged = pieces[m]
+        for j in range(devices):
+            if j != m:
+                shifted = pltpu.roll(pieces[j], (EIGHT * (j - m)) % LANES, 1)
+                merged = jnp.where(eighth == j, shifted, merged)
+        delta_ref[m * share : (m + 1) * share, last * LANES : (last + 1) * LANES] = merged
+    row = lax.broadcasted_iota(jnp.int32, (rows, width), 0)
+
+    def one(b, carry):
+        start = pl.multiple_of(position_ref[b] * rows, rows)
+        delta = jnp.where(row < used_ref[b], delta_ref[pl.ds(start, rows), :], 0.0)
+        out_ref[b] = (tokens_ref[b].astype(jnp.float32) + delta).astype(jnp.bfloat16)
+        return carry
+
+    lax.fori_loop(0, blocks, one, 0, unroll=4)
+
+
+def call(kernel, out_shape, in_specs, scratch, flops, moved):
+    return pl.pallas_call(
+        kernel,
+        out_shape=out_shape,
+        in_specs=in_specs,
+        out_specs=VMEM,
+        scratch_shapes=scratch,
+        compiler_params=pltpu.CompilerParams(vmem_limit_bytes=48 * 2**20),
+        cost_estimate=pl.CostEstimate(flops=flops, bytes_accessed=moved, transcendentals=0),
+    )
+
+
+def exchange(value):
+    return lax.all_to_all(value, "adapter", split_axis=0, concat_axis=0, tiled=True)
+
+
+def features_to_devices(
+    tokens, request_block_adapter, request_block_rows, adapter_down_weight, adapter_up_weight
+):
+    blocks, rows, width = tokens.shape
+    devices = lax.axis_size("adapter")
+    resident, unused_width, rank = adapter_down_weight.shape
+    slots = max(1, 4 * blocks // devices)
+    window = slots * rows
+    total = blocks * rows
+    weight_rows = resident // 2 * rank
+    bf16, f32, i32 = jnp.bfloat16, jnp.float32, jnp.int32
+
+    serial = jnp.arange(blocks, dtype=i32)
+    key = request_block_adapter * blocks + serial
+    position = jnp.sum(key[None, :] < key[:, None], axis=1).astype(i32)
+    ordered = jnp.sum(
+        jnp.where(position[:, None] == serial[None, :], request_block_adapter[:, None], 0), axis=0
+    ).astype(i32)
+    labels = lax.all_gather(ordered, "adapter")
+    holders = jnp.arange(devices, dtype=i32) * resident
+    starts = jnp.sum(labels[:, None, :] < holders[None, :, None], axis=2).astype(i32).reshape(-1)
+    labels = labels.reshape(-1)
+    group = lax.axis_index("groups").astype(i32).reshape(1)
+
+    def packed(count):
+        return jax.ShapeDtypeStruct((devices, count + count // 2 + count // devices, LANES), bf16)
+
+    size = devices * packed(total).shape[1] * LANES * 2
+    pack_weight = call(
+        functools.partial(weight_pack_kernel, devices, weight_rows),
+        packed(weight_rows),
+        [SMEM, VMEM],
+        [],
+        0,
+        3 * size,
+    )
+    down_share = exchange(
+        pack_weight(group, adapter_down_weight.transpose(0, 2, 1).reshape(resident * rank, width))
+    )
+    down_twin = lax.ppermute(down_share, "groups", [(0, 1), (1, 0)])
+    up_share = exchange(pack_weight(group, adapter_up_weight.reshape(resident * rank, width)))
+    up_twin = lax.ppermute(up_share, "groups", [(0, 1), (1, 0)])
+    outgoing = call(
+        functools.partial(token_pack_kernel, devices, total),
+        packed(total),
+        [SMEM, VMEM],
+        [pltpu.VMEM((total, width), f32)],
+        0,
+        2 * size,
+    )(position, tokens)
+    arrived = exchange(outgoing)
+
+    longest = total + window
+    flops = 2 * devices * devices * window * 2 * weight_rows * 2 * LANES
+    partial = call(
+        functools.partial(down_kernel, devices, blocks, rows, window, resident),
+        jax.ShapeDtypeStruct((devices, total // 2, LANES), f32),
+        [SMEM, SMEM, SMEM, VMEM, VMEM, VMEM],
+        [
+            pltpu.VMEM((devices, longest, 2 * LANES), f32),
+            pltpu.VMEM((devices, longest, LANES), f32),
+            pltpu.VMEM((devices, longest, LANES), i32),
+        ],
+        flops,
+        3 * size,
+    )(labels, starts, group, arrived, down_share, down_twin)
+    down = lax.psum(partial, "adapter")
+    leaving = call(
+        functools.partial(up_kernel, devices, blocks, rows, window, resident),
+        packed(total),
+        [SMEM, SMEM, SMEM, VMEM, VMEM, VMEM],
+        [
+            pltpu.VMEM((devices, longest, LANES), f32),
+            pltpu.VMEM((devices, longest, 2 * LANES), f32),
+            pltpu.VMEM((devices, longest, LANES), i32),
+        ],
+        flops,
+        3 * size,
+    )(labels, starts, group, down, up_share, up_twin)
+    returned = exchange(leaving)
+    return call(
+        functools.partial(mix_kernel, devices),
+        jax.ShapeDtypeStruct(tokens.shape, bf16),
+        [SMEM, SMEM, VMEM, VMEM],
+        [pltpu.VMEM((total, width), f32)],
+        0,
+        3 * size,
+    )(position, request_block_rows, tokens, returned)
+
+
 def solution(mesh):
     placed = (
         P(("groups", "adapter"), None, None),
@@ -75,6 +457,16 @@
         P("adapter", None, None),
         P("adapter", None, None),
     )
+
+    def per_device(tokens, request_block_adapter, request_block_rows, down_weight, up_weight):
+        devices = mesh.shape["adapter"]
+        even_deal = devices * EIGHT == LANES and tokens.shape[2] == devices * (
+            LANES + HALF + EIGHT
+        )
+        even_deal = even_deal and mesh.shape["groups"] == 2 and down_weight.shape[2] == HALF
+        plan = features_to_devices if even_deal else rows_to_holders
+        return plan(tokens, request_block_adapter, request_block_rows, down_weight, up_weight)
+
     return jax.shard_map(
         per_device,
         mesh=mesh,

time: 342 us -> 341 us (level)
  waiting for transfers between devices: 286 us -> 165 us
  blocking collectives: 0 us -> 76.7 us
  Pallas kernels: 0 us -> 58.6 us
  between operations: 0.05 us -> 14 us
  matrix products: 12.7 us -> 0 us
  local copies, waits for them, and re-layouts: 15.3 us -> 5.11 us
  other arithmetic: 9.71 us -> 0.69 us
    all_to_all x3, waiting for transfers between devices: 286 us -> 71.9 us  [exchange(): lax.all_to_all(value, 'adapter', split_axis=0, concat_axis=0, tiled=True)]
    psum x0 -> x1, waiting for transfers between devices: none -> 88.6 us  [features_to_devices(): down = lax.psum(partial, 'adapter')]
    pallas_call x0 -> x6, Pallas kernels: none -> 58.6 us  [the longest x1 29.3 us: features_to_devices(): call(functools.partial(down_kernel, devices, blocks, rows, window, reside...]
    all_to_all x0 -> x1, blocking collectives: none -> 44.1 us  [exchange(): lax.all_to_all(value, 'adapter', split_axis=0, concat_axis=0, tiled=True)]
    unnamed x0 -> x1, blocking collectives: none -> 32.5 us
    unnamed x1 -> x0, matrix products: 6.85 us -> none
    convert_element_type x2 -> x0, other arithmetic: 6.78 us -> none  [the longest x1 3.76 us: per_device(): return mixed.astype(jnp.bfloat16)]
    scatter x2 -> x0, local copies, waits for them, and re-layouts: 6.54 us -> none  [the longest x1 5.86 us: per_device(): jnp.zeros((devices * slots, rows, feature_width), jnp.bfloat16).at[position]]
  transfers between devices with their start and end apart: 3 -> 6, of which waited for: 2 -> 5; matrix products, arithmetic and copies ran while one was open for 4% -> 0% of each run, Pallas kernels for 0% -> 10%
where the time goes in v1:
time: 341 us; the launch traced here: 338 us
  waiting for transfers between devices  165 us (48%)
  blocking collectives  76.7 us (22%)
  Pallas kernels  58.6 us (17%)
  starting transfers between devices  18.2 us (5%)
  between operations  14 us (4%)
  local copies, waits for them, and re-layouts  5.11 us (1%)
    psum x1, waiting for transfers between devices, features_to_devices(): down = lax.psum(partial, 'adapter')  88.6 us
    all_to_all x3, waiting for transfers between devices, exchange(): lax.all_to_all(value, 'adapter', split_axis=0, concat_axis=0, tiled=True)  71.9 us
    all_to_all x1, blocking collectives, exchange(): lax.all_to_all(value, 'adapter', split_axis=0, concat_axis=0, tiled=True)  44.1 us
    unnamed x1, blocking collectives  32.5 us
    pallas_call x1, Pallas kernels, features_to_devices(): call(functools.partial(down_kernel, devices, blocks, rows, window, reside...  29.3 us
    pallas_call x1, Pallas kernels, features_to_devices(): call(functools.partial(up_kernel, devices, blocks, rows, window, resident...  19.7 us
    all_to_all x3, starting transfers between devices, exchange(): lax.all_to_all(value, 'adapter', split_axis=0, concat_axis=0, tiled=True)  16.6 us
  transfers between devices with their start and end apart: 6, of which 5 were waited for; matrix products, arithmetic and copies ran while one was open for 0% of the time, Pallas kernels for 10%

profile of v1, /device:TPU:11, one launch (start us, length us, event | category | flops | bytes accessed | tf_op | source)
XLA Modules:
  0.0 338.0 jit_solution(15305058140519048196)
XLA Ops:
  6.5 1.9 copy-done.1
  8.5 1.8 shard_map.56
  10.2 6.8 %all-to-all-start.1 = ((bf16[16,400,128]{2,1,0:T(8,128)(2,1)}), bf16[16,400,128]{2,1,0:T(8,128)(2,1)}, u32[]{:S(2)}, u32[]{:S(2)}) async-start(bf16[16,400,128]{2,1,0:T(8,128)(2,1)} %shard_map.56), calls=%async_computation.1 | async-start | bytes 3276800 | tf_op jit(solution)/shard_map/all_to_all | solution.py:359
  17.0 1.8 shard_map.58
  18.8 35.9 %all-to-all-done.1.own_ref = bf16[16,400,128]{2,1,0:T(8,128)(2,1)} async-done(((bf16[16,400,128]{2,1,0:T(8,128)(2,1)}), bf16[16,400,128]{2,1,0:T(8,128)(2,1)}, u32[]{:S(2)}, u32[]{:S(2)}) %all-to-all-start.1) | async-done | bytes 1638432 | tf_op jit(solution)/shard_map/all_to_all | solution.py:359
  54.7 4.9 %all-to-all-start.2 = ((bf16[16,400,128]{2,1,0:T(8,128)(2,1)}), bf16[16,400,128]{2,1,0:T(8,128)(2,1)S(1)}, u32[]{:S(2)}, u32[]{:S(2)}) async-start(bf16[16,400,128]{2,1,0:T(8,128)(2,1)} %shard_map.58), calls=%async_computation.2 | async-start | bytes 3276800 | tf_op jit(solution)/shard_map/all_to_all | solution.py:359
  59.8 3.4 shard_map.55
  63.2 34.0 %all-to-all-done.2.own_ref = bf16[16,400,128]{2,1,0:T(8,128)(2,1)S(1)} async-done(((bf16[16,400,128]{2,1,0:T(8,128)(2,1)}), bf16[16,400,128]{2,1,0:T(8,128)(2,1)S(1)}, u32[]{:S(2)}, u32[]{:S(2)}) %all-to-all-start.2) | async-done | bytes 1638432 | tf_op jit(solution)/shard_map/all_to_all | solution.py:359
  97.2 4.9 %all-to-all-start = ((bf16[16,400,128]{2,1,0:T(8,128)(2,1)}), bf16[16,400,128]{2,1,0:T(8,128)(2,1)}, u32[]{:S(2)}, u32[]{:S(2)}) async-start(bf16[16,400,128]{2,1,0:T(8,128)(2,1)} %shard_map.55), calls=%async_computation | async-start | bytes 3276800 | tf_op jit(solution)/shard_map/all_to_all | solution.py:359
  102.2 1.3 collective-permute-start
  103.5 0.2 collective-permute-start.1
  103.7 0.6 dynamic-slice
  105.0 0.2 dynamic-update-slice
  105.2 32.5 %all-reduce.labels_ref = s32[512]{0:T(512)S(1)} all-reduce(s32[512]{0:T(512)S(1)} %dynamic-update-slice), channel_id=2, replica_groups=mesh['groups'=2,'adapter'=16] {'adapter'}, use_global_device_ids=true, to_apply=%add | all-reduce | flops 512 | bytes 4096
  137.8 0.4 convert_reduce_fusion
  138.3 1.9 all-to-all-done.rows_ref
  140.3 29.3 %shard_map.57 = f32[16,128,128]{2,1,0:T(8,128)S(1)} custom-call(s32[512]{0:T(512)S(1)} %all-reduce.labels_ref, s32[256]{0:T(256)S(1)} %reshape.25.starts_ref, s32[1]{0:T(128)} %bitcast.1.which_ref.group_ref, bf16[16,400,128]{2,1,0:T(8,128)(2,1)} %all-to-all-done.rows_ref, bf16[16,400,128]{2,1,0:T(8,128)(2,1)} %all-to-all-done.1.own_ref, ...), custom_call_target="tpu_custom_call" | custom-call | flops 4294967296 | bytes 4915200 | tf_op jit(solution)/shard_map/pallas_call | solution.py:416
  169.6 1.0 copy-done.3
  170.6 4.1 %collective-permute-done.1.twin_ref = bf16[16,400,128]{2,1,0:T(8,128)(2,1)} collective-permute-done((bf16[16,400,128]{2,1,0:T(8,128)(2,1)S(1)}, bf16[16,400,128]{2,1,0:T(8,128)(2,1)}, u32[]{:S(2)}, u32[]{:S(2)}) %collective-permute-start.1) | collective-permute-done | bytes 1638432 | tf_op jit(solution)/shard_map/ppermute | solution.py:403
  174.7 88.6 %all-reduce.3.cloned.1.call-done.down_ref = f32[16,128,128]{2,1,0:T(8,128)} async-done(((f32[16,128,128]{2,1,0:T(8,128)}), f32[16,128,128]{2,1,0:T(8,128)}) %all-reduce.3.cloned.1.call-update) | async-done | bytes 1048592 | tf_op jit(solution)/shard_map/psum | solution.py:428
  263.3 1.2 copy-done.5
  264.5 19.7 %shard_map.59 = bf16[16,400,128]{2,1,0:T(8,128)(2,1)S(1)} custom-call(s32[512]{0:T(512)S(1)} %all-reduce.labels_ref, s32[256]{0:T(256)S(1)} %reshape.25.starts_ref, s32[1]{0:T(128)} %bitcast.1.which_ref.group_ref, f32[16,128,128]{2,1,0:T(8,128)S(1)} %copy-done.5, bf16[16,400,128]{2,1,0:T(8,128)(2,1)S(1)} %all-to-all-done.2.own_ref, ...), custom_call_target="tpu_custom_call" | custom-call | flops 4294967296 | bytes 4915200 | tf_op jit(solution)/shard_map/pallas_call | solution.py:429
  284.3 44.1 %all_to_all.20.returned_ref = bf16[16,400,128]{2,1,0:T(8,128)(2,1)S(1)} all-to-all(bf16[16,400,128]{2,1,0:T(8,128)(2,1)S(1)} %shard_map.59), channel_id=1, replica_groups=mesh['groups'=2,'adapter'=16] {'adapter'}, dimensions={0} | all-to-all | bytes 3276800 | tf_op jit(solution)/shard_map/all_to_all | solution.py:359
  328.4 2.7 shard_map.60
  (23 shorter events, 0.5 us)
Async XLA Ops:
  6.5 1.9 copy-start.1
  10.2 6.8 %copy-start.2 = (bf16[8,64,3200]{2,1,0:T(8,128)(2,1)S(1)}, bf16[8,64,3200]{2,1,0:T(8,128)(2,1)}, u32[]{:S(2)}) copy-start(bf16[8,64,3200]{2,1,0:T(8,128)(2,1)} %param.9) | copy-start | bytes 9830404
  10.2 44.5 %all-to-all-start.1 = ((bf16[16,400,128]{2,1,0:T(8,128)(2,1)}), bf16[16,400,128]{2,1,0:T(8,128)(2,1)}, u32[]{:S(2)}, u32[]{:S(2)}) async-start(bf16[16,400,128]{2,1,0:T(8,128)(2,1)} %shard_map.56), calls=%async_computation.1 | async-start | bytes 3276800 | tf_op jit(solution)/shard_map/all_to_all | solution.py:359
  18.8 40.8 %copy-start.6 = (s32[32]{0:T(128)S(1)}, s32[32]{0:T(128)}, u32[]{:S(2)}) copy-start(s32[32]{0:T(128)} %param.6) | copy-start | bytes 388
  18.8 41.0 %copy-start = (bf16[32,8,3200]{2,1,0:T(8,128)(2,1)S(1)}, bf16[32,8,3200]{2,1,0:T(8,128)(2,1)}, u32[]{:S(2)}) copy-start(bf16[32,8,3200]{2,1,0:T(8,128)(2,1)} %tokens_ref.3) | copy-start | bytes 4915204
  54.7 42.5 %all-to-all-start.2 = ((bf16[16,400,128]{2,1,0:T(8,128)(2,1)}), bf16[16,400,128]{2,1,0:T(8,128)(2,1)S(1)}, u32[]{:S(2)}, u32[]{:S(2)}) async-start(bf16[16,400,128]{2,1,0:T(8,128)(2,1)} %shard_map.58), calls=%async_computation.2 | async-start | bytes 3276800 | tf_op jit(solution)/shard_map/all_to_all | solution.py:359
  63.2 40.5 %copy-start.7 = (u32[32]{0:T(128)S(1)}, u32[32]{0:T(128)}, u32[]{:S(2)}) copy-start(u32[32]{0:T(128)} %constant.16) | copy-start | bytes 388
  97.2 43.0 %all-to-all-start = ((bf16[16,400,128]{2,1,0:T(8,128)(2,1)}), bf16[16,400,128]{2,1,0:T(8,128)(2,1)}, u32[]{:S(2)}, u32[]{:S(2)}) async-start(bf16[16,400,128]{2,1,0:T(8,128)(2,1)} %shard_map.55), calls=%async_computation | async-start | bytes 3276800 | tf_op jit(solution)/shard_map/all_to_all | solution.py:359
  102.1 161.2 %all-reduce.3.cloned.1.call-start = ((), (), s32[]{:S(2)}) async-start(), calls=%async_computation.4 | async-start | bytes 2097152 | tf_op jit(solution)/shard_map/psum | solution.py:428
  102.2 38.1 %collective-permute-start = (bf16[16,400,128]{2,1,0:T(8,128)(2,1)}, bf16[16,400,128]{2,1,0:T(8,128)(2,1)}, u32[]{:S(2)}, u32[]{:S(2)}) collective-permute-start(bf16[16,400,128]{2,1,0:T(8,128)(2,1)} %all-to-all-done.1.own_ref), channel_id=1, source_target_pairs={{0,16},{16,0},{1,17},{17,1},{2,18},{18,2},{3,19},{19,3},{4,20},{20... | collective-permute-start | bytes 4915208 | tf_op jit(solution)/shard_map/ppermute | solution.py:401
  103.5 71.2 %collective-permute-start.1 = (bf16[16,400,128]{2,1,0:T(8,128)(2,1)S(1)}, bf16[16,400,128]{2,1,0:T(8,128)(2,1)}, u32[]{:S(2)}, u32[]{:S(2)}) collective-permute-start(bf16[16,400,128]{2,1,0:T(8,128)(2,1)S(1)} %all-to-all-done.2.own_ref), channel_id=1, source_target_pairs={{0,16},{16,0},{1,17},{17,1},{2,18},{18,2},{3,19},{19,3},{4,20},{20... | collective-permute-start | bytes 4915208 | tf_op jit(solution)/shard_map/ppermute | solution.py:403
  169.6 1.0 copy-start.3
  263.3 1.2 copy-start.5
  284.3 44.2 %copy-start.4 = (s32[32]{0:T(128)S(1)}, s32[32]{0:T(128)}, u32[]{:S(2)}) copy-start(s32[32]{0:T(128)} %used_ref.1) | copy-start | bytes 388
Sparse Core Ops, SparseCore 0:
  170.7 92.5 all-reduce.2

commit v2 on v1

--- a/solution.py
+++ b/solution.py
@@ -81,18 +81,23 @@
     return lax.broadcasted_iota(jnp.int32, (rows, LANES), 1)
 
 
-def pack_all(read, out_ref, devices, total):
+def share_rows(total, devices):
+    return total + total // 2 + total // devices
+
+
+def pack_all(read, out_ref, devices, total, base):
     half, part = total // 2, total // devices
     low = lanes_of(half) < HALF
+    at_half, at_part = base + total, base + total + half
     for j in range(devices):
-        out_ref[j, 0:total, :] = read(0, total, j).astype(jnp.bfloat16)
+        out_ref[j, base : base + total, :] = read(0, total, j).astype(jnp.bfloat16)
     for i in range(devices // 2):
         upper = read(0, half, devices + i).astype(jnp.float32)
         lower = read(half, half, devices + i).astype(jnp.float32)
         even = jnp.where(low, upper, pltpu.roll(lower, HALF, 1))
         odd = jnp.where(low, pltpu.roll(upper, HALF, 1), lower)
-        out_ref[2 * i, total : total + half, :] = even.astype(jnp.bfloat16)
-        out_ref[2 * i + 1, total : total + half, :] = odd.astype(jnp.bfloat16)
+        out_ref[2 * i, at_half : at_half + half, :] = even.astype(jnp.bfloat16)
+        out_ref[2 * i + 1, at_half : at_half + half, :] = odd.astype(jnp.bfloat16)
     last = devices + devices // 2
     group = lanes_of(part) // EIGHT
     pieces = [read(m * part, part, last).astype(jnp.float32) for m in range(devices)]
@@ -102,13 +107,14 @@
             if m != j:
                 shifted = pltpu.roll(pieces[m], (EIGHT * (m - j)) % LANES, 1)
                 merged = jnp.where(group == m, shifted, merged)
-        out_ref[j, total + half : total + half + part, :] = merged.astype(jnp.bfloat16)
-
-
-def unpack_second(share, devices, total):
+        out_ref[j, at_part : at_part + part, :] = merged.astype(jnp.bfloat16)
+
+
+def unpack_second(share, devices, total, base=0):
     half, part = total // 2, total // devices
-    first = share[total : total + half, :].astype(jnp.float32)
-    rest = share[total + half : total + half + part, :].astype(jnp.float32)
+    at_half, at_part = base + total, base + total + half
+    first = share[at_half : at_half + half, :].astype(jnp.float32)
+    rest = share[at_part : at_part + part, :].astype(jnp.float32)
     halves = jnp.concatenate([first, pltpu.roll(first, HALF, 1)], axis=0)
     eights = jnp.concatenate(
         [pltpu.roll(rest, (HALF - EIGHT * m) % LANES, 1) for m in range(devices)], axis=0
@@ -116,16 +122,23 @@
     return jnp.where(lanes_of(total) < HALF, halves, eights)
 
 
+def weight_of(ref, h, devices, weight_rows, base=0):
+    second = unpack_second(ref.at[h], devices, weight_rows, base).astype(jnp.bfloat16)
+    return jnp.concatenate([ref[h, base : base + weight_rows, :], second], axis=1)
+
+
 def weight_pack_kernel(devices, total, which_ref, weight_ref, out_ref):
     start = pl.multiple_of(which_ref[0] * total, total)
 
     def read(row, count, tile):
         return weight_ref[pl.ds(start + row, count), tile * LANES : (tile + 1) * LANES]
 
-    pack_all(read, out_ref, devices, total)
-
-
-def token_pack_kernel(devices, total, position_ref, tokens_ref, out_ref, sorted_ref):
+    pack_all(read, out_ref, devices, total, 0)
+
+
+def first_pack_kernel(
+    devices, total, weight_rows, which_ref, position_ref, tokens_ref, weight_ref, out_ref, sorted_ref
+):
     blocks, rows, width = tokens_ref.shape
 
     def one(b, carry):
@@ -137,10 +150,16 @@
 
     lax.fori_loop(0, blocks, one, 0, unroll=4)
 
-    def read(row, count, tile):
+    def read_rows(row, count, tile):
         return sorted_ref[row : row + count, tile * LANES : (tile + 1) * LANES]
 
-    pack_all(read, out_ref, devices, total)
+    pack_all(read_rows, out_ref, devices, total, 0)
+    start = pl.multiple_of(which_ref[0] * weight_rows, weight_rows)
+
+    def read_weight(row, count, tile):
+        return weight_ref[pl.ds(start + row, count), tile * LANES : (tile + 1) * LANES]
+
+    pack_all(read_weight, out_ref, devices, weight_rows, share_rows(total, devices))
 
 
 def fill_labels(devices, blocks, rows, labels_ref, label_rows_ref):
@@ -168,22 +187,24 @@
     labels_ref,
     starts_ref,
     group_ref,
-    rows_ref,
-    own_ref,
+    first_ref,
     twin_ref,
     out_ref,
     spread_ref,
     sum_ref,
     label_rows_ref,
+    batch_ref,
+    product_ref,
 ):
     total = blocks * rows
     weight_rows = resident // 2 * HALF
+    batch = total // window
     fill_labels(devices, blocks, rows, labels_ref, label_rows_ref)
     inside = lanes_of(total) < HALF + EIGHT
 
     def spread(s, carry):
-        spread_ref[s, 0:total, 0:LANES] = rows_ref[s, 0:total, :].astype(jnp.float32)
-        second = unpack_second(rows_ref.at[s], devices, total)
+        spread_ref[s, 0:total, 0:LANES] = first_ref[s, 0:total, :].astype(jnp.float32)
+        second = unpack_second(first_ref.at[s], devices, total)
         spread_ref[s, 0:total, LANES:] = jnp.where(inside, second, 0.0)
         spread_ref[s, total : total + window, :] = jnp.zeros((window, 2 * LANES), jnp.float32)
         return carry
@@ -193,26 +214,35 @@
     own_at = group * (resident // 2)
     twin_at = (1 - group) * (resident // 2)
     upper = (lanes_of(window) >= HALF).astype(jnp.int32)
-
-    def weight_of(ref, h):
-        second = unpack_second(ref.at[h], devices, weight_rows).astype(jnp.bfloat16)
-        return jnp.concatenate([ref[h, 0:weight_rows, :], second], axis=1)
+    dims = (((1,), (1,)), ((), ()))
 
     def holder(h, carry):
-        own = weight_of(own_ref, h)
-        twin = weight_of(twin_ref, h)
+        own = weight_of(first_ref, h, devices, weight_rows, share_rows(total, devices))
+        twin = weight_of(twin_ref, h, devices, weight_rows)
+        both = jnp.concatenate([own, twin], axis=0)
+
+        def start_of(s):
+            return pl.multiple_of(starts_ref[s * devices + h] * rows, rows)
+
         for s in range(devices):
-            start = pl.multiple_of(starts_ref[s * devices + h] * rows, rows)
-            part = spread_ref[s, pl.ds(start, window), :].astype(jnp.bfloat16)
+            batch_ref[s * window : (s + 1) * window, :] = spread_ref[
+                s, pl.ds(start_of(s), window), :
+            ].astype(jnp.bfloat16)
+        for c in range(devices // batch):
+            piece = slice(c * total, (c + 1) * total)
+            product_ref[piece, :] = lax.dot_general(
+                batch_ref[piece, :], both, dims, preferred_element_type=jnp.float32
+            )
+        for s in range(devices):
+            start = start_of(s)
             label = label_rows_ref[s, pl.ds(start, window), :] - h * resident - upper
-            dims = (((1,), (1,)), ((), ()))
-            mine = lax.dot_general(part, own, dims, preferred_element_type=jnp.float32)
-            other = lax.dot_general(part, twin, dims, preferred_element_type=jnp.float32)
             picked = jnp.zeros((window, LANES), jnp.float32)
-            for t in range(resident // 4):
-                columns = slice(t * LANES, (t + 1) * LANES)
-                picked = jnp.where(label == own_at + 2 * t, mine[:, columns], picked)
-                picked = jnp.where(label == twin_at + 2 * t, other[:, columns], picked)
+            for t in range(resident // 2):
+                at = own_at + 2 * t if t < resident // 4 else twin_at + 2 * t - resident // 2
+                product = product_ref[
+                    s * window : (s + 1) * window, t * LANES : (t + 1) * LANES
+                ]
+                picked = jnp.where(label == at, product, picked)
             sum_ref[s, pl.ds(start, window), :] = picked + pltpu.roll(picked, HALF, 1)
         return carry
 
@@ -226,6 +256,15 @@
         return carry
 
     lax.fori_loop(0, devices, leave, 0)
+
+
+def add_kernel(devices, parts_ref, out_ref):
+    total = parts_ref[0].astype(jnp.float32)
+    for j in range(1, devices):
+        total = total + parts_ref[j].astype(jnp.float32)
+    rounded = total.astype(jnp.bfloat16)
+    for j in range(devices):
+        out_ref[j] = rounded
 
 
 def up_kernel(
@@ -244,15 +283,17 @@
     twice_ref,
     delta_ref,
     label_rows_ref,
+    batch_ref,
 ):
     total = blocks * rows
     half, share = total // 2, total // devices
     weight_rows = resident // 2 * HALF
+    batch = total // window
     fill_labels(devices, blocks, rows, labels_ref, label_rows_ref)
     low = lanes_of(half) < HALF
 
     def spread(s, carry):
-        packed = down_ref[s].astype(jnp.bfloat16).astype(jnp.float32)
+        packed = down_ref[s].astype(jnp.float32)
         turned = pltpu.roll(packed, HALF, 1)
         twice_ref[s, 0:half, :] = jnp.where(low, packed, turned)
         twice_ref[s, half:total, :] = jnp.where(low, turned, packed)
@@ -265,26 +306,32 @@
     twin_at = (1 - group) * (resident // 2)
     upper = (lanes_of(window) >= HALF).astype(jnp.int32)
 
-    def weight_of(ref, h):
-        second = unpack_second(ref.at[h], devices, weight_rows).astype(jnp.bfloat16)
-        return jnp.concatenate([ref[h, 0:weight_rows, :], second], axis=1)
-
     def holder(h, carry):
-        own = weight_of(own_ref, h)
-        twin = weight_of(twin_ref, h)
+        own = weight_of(own_ref, h, devices, weight_rows)
+        twin = weight_of(twin_ref, h, devices, weight_rows)
+        both = jnp.concatenate([own, twin], axis=0)
+
+        def start_of(s):
+            return pl.multiple_of(starts_ref[s * devices + h] * rows, rows)
+
         for s in range(devices):
-            start = pl.multiple_of(starts_ref[s * devices + h] * rows, rows)
+            start = start_of(s)
             part = twice_ref[s, pl.ds(start, window), :]
             label = label_rows_ref[s, pl.ds(start, window), :] - h * resident - upper
-            sides = []
-            for at in (own_at, twin_at):
-                placed = [
-                    jnp.where(label == at + 2 * t, part, 0.0) for t in range(resident // 4)
+            for t in range(resident // 2):
+                at = own_at + 2 * t if t < resident // 4 else twin_at + 2 * t - resident // 2
+                batch_ref[s * window : (s + 1) * window, t * LANES : (t + 1) * LANES] = jnp.where(
+                    label == at, part, 0.0
+                ).astype(jnp.bfloat16)
+        for c in range(devices // batch):
+            product = jnp.dot(
+                batch_ref[c * total : (c + 1) * total, :], both, preferred_element_type=jnp.float32
+            )
+            for i in range(batch):
+                s = c * batch + i
+                delta_ref[s, pl.ds(start_of(s), window), :] = product[
+                    i * window : (i + 1) * window
                 ]
-                sides.append(jnp.concatenate(placed, axis=1).astype(jnp.bfloat16))
-            delta_ref[s, pl.ds(start, window), :] = jnp.dot(
-                sides[0], own, preferred_element_type=jnp.float32
-            ) + jnp.dot(sides[1], twin, preferred_element_type=jnp.float32)
         return carry
 
     lax.fori_loop(0, devices, holder, 0)
@@ -359,6 +406,19 @@
     return lax.all_to_all(value, "adapter", split_axis=0, concat_axis=0, tiled=True)
 
 
+def gather_labels(ordered, devices):
+    held = ordered[None]
+    step = 1
+    while step < devices:
+        pairs = [(i, i ^ step) for i in range(devices)]
+        held = jnp.concatenate([held, lax.ppermute(held, "adapter", pairs)], axis=0)
+        step *= 2
+    serial = jnp.arange(devices, dtype=jnp.int32)
+    source = jnp.bitwise_xor(lax.axis_index("adapter").astype(jnp.int32), serial)
+    chosen = source[:, None] == serial[None, :]
+    return jnp.sum(jnp.where(chosen[:, :, None], held[None], 0), axis=1)
+
+
 def features_to_devices(
     tokens, request_block_adapter, request_block_rows, adapter_down_weight, adapter_up_weight
 ):
@@ -377,63 +437,71 @@
     ordered = jnp.sum(
         jnp.where(position[:, None] == serial[None, :], request_block_adapter[:, None], 0), axis=0
     ).astype(i32)
-    labels = lax.all_gather(ordered, "adapter")
+    labels = gather_labels(ordered, devices)
     holders = jnp.arange(devices, dtype=i32) * resident
     starts = jnp.sum(labels[:, None, :] < holders[None, :, None], axis=2).astype(i32).reshape(-1)
     labels = labels.reshape(-1)
     group = lax.axis_index("groups").astype(i32).reshape(1)
 
-    def packed(count):
-        return jax.ShapeDtypeStruct((devices, count + count // 2 + count // devices, LANES), bf16)
-
-    size = devices * packed(total).shape[1] * LANES * 2
-    pack_weight = call(
+    def shares(count):
+        return jax.ShapeDtypeStruct((devices, count, LANES), bf16)
+
+    row_share, weight_share = share_rows(total, devices), share_rows(weight_rows, devices)
+    size = devices * row_share * LANES * 2
+    outgoing = call(
+        functools.partial(first_pack_kernel, devices, total, weight_rows),
+        shares(row_share + weight_share),
+        [SMEM, SMEM, VMEM, VMEM],
+        [pltpu.VMEM((total, width), f32)],
+        0,
+        4 * size,
+    )(group, position, tokens, adapter_down_weight.transpose(0, 2, 1).reshape(-1, width))
+    first = exchange(outgoing)
+    swap = [(0, 1), (1, 0)]
+    down_twin = lax.ppermute(first[:, row_share:, :], "groups", swap)
+    up_packed = call(
         functools.partial(weight_pack_kernel, devices, weight_rows),
-        packed(weight_rows),
+        shares(weight_share),
         [SMEM, VMEM],
         [],
         0,
         3 * size,
-    )
-    down_share = exchange(
-        pack_weight(group, adapter_down_weight.transpose(0, 2, 1).reshape(resident * rank, width))
-    )
-    down_twin = lax.ppermute(down_share, "groups", [(0, 1), (1, 0)])
-    up_share = exchange(pack_weight(group, adapter_up_weight.reshape(resident * rank, width)))
-    up_twin = lax.ppermute(up_share, "groups", [(0, 1), (1, 0)])
-    outgoing = call(
-        functools.partial(token_pack_kernel, devices, total),
-        packed(total),
-        [SMEM, VMEM],
-        [pltpu.VMEM((total, width), f32)],
-        0,
-        2 * size,
-    )(position, tokens)
-    arrived = exchange(outgoing)
+    )(group, adapter_up_weight.reshape(-1, width))
+    up_packed, first = lax.optimization_barrier((up_packed, first))
+    up_share = exchange(up_packed)
+    up_twin = lax.ppermute(up_share, "groups", swap)
 
     longest = total + window
-    flops = 2 * devices * devices * window * 2 * weight_rows * 2 * LANES
+    columns = resident * rank
+    flops = 2 * devices * devices * window * columns * 2 * LANES
+    label_rows = pltpu.VMEM((devices, longest, LANES), i32)
     partial = call(
         functools.partial(down_kernel, devices, blocks, rows, window, resident),
-        jax.ShapeDtypeStruct((devices, total // 2, LANES), f32),
-        [SMEM, SMEM, SMEM, VMEM, VMEM, VMEM],
+        shares(total // 2),
+        [SMEM, SMEM, SMEM, VMEM, VMEM],
         [
             pltpu.VMEM((devices, longest, 2 * LANES), f32),
             pltpu.VMEM((devices, longest, LANES), f32),
-            pltpu.VMEM((devices, longest, LANES), i32),
+            label_rows,
+            pltpu.VMEM((devices * window, 2 * LANES), bf16),
+            pltpu.VMEM((devices * window, columns), f32),
         ],
         flops,
         3 * size,
-    )(labels, starts, group, arrived, down_share, down_twin)
-    down = lax.psum(partial, "adapter")
+    )(labels, starts, group, first, down_twin)
+    summed = call(
+        functools.partial(add_kernel, devices), shares(total // 2), [VMEM], [], 0, size
+    )(exchange(partial))
+    down = exchange(summed)
     leaving = call(
         functools.partial(up_kernel, devices, blocks, rows, window, resident),
-        packed(total),
+        shares(row_share),
         [SMEM, SMEM, SMEM, VMEM, VMEM, VMEM],
         [
             pltpu.VMEM((devices, longest, LANES), f32),
             pltpu.VMEM((devices, longest, 2 * LANES), f32),
-            pltpu.VMEM((devices, longest, LANES), i32),
+            label_rows,
+            pltpu.VMEM((devices * window, columns), bf16),
         ],
         flops,
         3 * size,

time: 341 us -> 257 us (0.75)
  waiting for transfers between devices: 165 us -> 119 us
  Pallas kernels: 58.6 us -> 37 us
  blocking collectives: 76.7 us -> 62.7 us
  between operations: 14 us -> 0.12 us
  starting transfers between devices: 18.2 us -> 23.1 us
  local copies, waits for them, and re-layouts: 5.11 us -> 9.38 us
    psum x1 -> x0, waiting for transfers between devices: 88.6 us -> none  [features_to_devices(): down = lax.psum(partial, 'adapter')]
    ppermute x2 -> x6, waiting for transfers between devices: 4.13 us -> 37.8 us  [the longest x4 30.6 us: gather_labels(): held = jnp.concatenate([held, lax.ppermute(held, 'adapter', pairs)], axis=0)]
    unnamed x1 -> x0, blocking collectives: 32.5 us -> none
    all_to_all x1 -> x2, blocking collectives: 44.1 us -> 62.7 us  [exchange(): lax.all_to_all(value, 'adapter', split_axis=0, concat_axis=0, tiled=True)]
    pallas_call x1, Pallas kernels: 29.3 us -> 13.7 us  [features_to_devices(): call(functools.partial(down_kernel, devices, blocks, rows, window, reside...]
    all_to_all x3, waiting for transfers between devices: 71.9 us -> 81.6 us  [exchange(): lax.all_to_all(value, 'adapter', split_axis=0, concat_axis=0, tiled=True)]
    pallas_call x1, Pallas kernels: 19.7 us -> 14 us  [features_to_devices(): call(functools.partial(up_kernel, devices, blocks, rows, window, resident...]
    unnamed x19 -> x18, local copies, waits for them, and re-layouts: 4.95 us -> 7.93 us
  transfers between devices with their start and end apart: 6 -> 9, of which waited for: 5 -> 8; matrix products, arithmetic and copies ran while one was open for 0% -> 1% of each run, Pallas kernels for 10% -> 6%
where the time goes in v2:
time: 257 us; the launch traced here: 253 us
  waiting for transfers between devices  119 us (46%)
  blocking collectives  62.7 us (24%)
  Pallas kernels  37 us (14%)
  starting transfers between devices  23.1 us (9%)
  local copies, waits for them, and re-layouts  9.38 us (4%)
    all_to_all x3, waiting for transfers between devices, exchange(): lax.all_to_all(value, 'adapter', split_axis=0, concat_axis=0, tiled=True)  81.6 us
    all_to_all x2, blocking collectives, exchange(): lax.all_to_all(value, 'adapter', split_axis=0, concat_axis=0, tiled=True)  62.7 us
    ppermute x4, waiting for transfers between devices, gather_labels(): held = jnp.concatenate([held, lax.ppermute(held, 'adapter', pairs)], axis=0)  30.6 us
    all_to_all x3, starting transfers between devices, exchange(): lax.all_to_all(value, 'adapter', split_axis=0, concat_axis=0, tiled=True)  18.3 us
    pallas_call x1, Pallas kernels, features_to_devices(): call(functools.partial(up_kernel, devices, blocks, rows, window, resident...  14 us
    pallas_call x1, Pallas kernels, features_to_devices(): call(functools.partial(down_kernel, devices, blocks, rows, window, reside...  13.7 us
    unnamed x18, local copies, waits for them, and re-layouts  7.93 us
    pallas_call x1, Pallas kernels, features_to_devices(): call(functools.partial(first_pack_kernel, devices, total, weight_rows), s...  5.89 us
  transfers between devices with their start and end apart: 9, of which 8 were waited for; matrix products, arithmetic and copies ran while one was open for 1% of the time, Pallas kernels for 6%

profile of v2, /device:TPU:11, one launch (start us, length us, event | category | flops | bytes accessed | tf_op | source)
XLA Modules:
  0.0 253.2 jit_solution(15387196522067876472)
XLA Ops:
  0.8 1.4 copy-done.1
  2.3 5.9 %shard_map.56 = bf16[16,800,128]{2,1,0:T(8,128)(2,1)} custom-call(s32[1]{0:T(128)} %bitcast.1.which_ref.group_ref, s32[32]{0:T(128)S(1)} %convert_reduce_fusion.1.position_ref, bf16[32,8,3200]{2,1,0:T(8,128)(2,1)S(1)} %copy-done.1, bf16[512,3200]{1,0:T(8,128)(2,1)} %bitcast.7), custom_call_target="tpu_custom_call" | custom-call | bytes 6553600 | tf_op jit(solution)/shard_map/pallas_call | solution.py:451
  8.2 6.6 %all-to-all-start = ((bf16[16,800,128]{2,1,0:T(8,128)(2,1)}), bf16[16,800,128]{2,1,0:T(8,128)(2,1)S(1)}, u32[]{:S(2)}, u32[]{:S(2)}) async-start(bf16[16,800,128]{2,1,0:T(8,128)(2,1)} %shard_map.56), calls=%async_computation | async-start | bytes 6553600 | tf_op jit(solution)/shard_map/all_to_all | solution.py:406
  14.7 1.9 copy-done.3
  17.3 1.2 copy-done
  18.4 69.0 %all-to-all-done.first_ref = bf16[16,800,128]{2,1,0:T(8,128)(2,1)S(1)} async-done(((bf16[16,800,128]{2,1,0:T(8,128)(2,1)}), bf16[16,800,128]{2,1,0:T(8,128)(2,1)S(1)}, u32[]{:S(2)}, u32[]{:S(2)}) %all-to-all-start) | async-done | bytes 3276832 | tf_op jit(solution)/shard_map/all_to_all | solution.py:406
  87.4 4.9 %all-to-all-start.3 = ((bf16[16,400,128]{2,1,0:T(8,128)(2,1)}), bf16[16,400,128]{2,1,0:T(8,128)(2,1)}, u32[]{:S(2)}, u32[]{:S(2)}) async-start(bf16[16,400,128]{2,1,0:T(8,128)(2,1)} %copy-done), calls=%async_computation.3 | async-start | bytes 3276800 | tf_op jit(solution)/shard_map/all_to_all | solution.py:406
  92.3 1.3 slice.4
  93.6 1.2 collective-permute-start.4
  96.8 3.5 %collective-permute-done.1 = s32[2,32]{1,0:T(2,128)S(1)} collective-permute-done((s32[2,32]{1,0:T(2,128)S(1)}, s32[2,32]{1,0:T(2,128)S(1)}, u32[]{:S(2)}, u32[]{:S(2)}) %collective-permute-start.1) | collective-permute-done | bytes 288 | tf_op jit(solution)/shard_map/ppermute | solution.py:414
  100.5 19.8 %collective-permute-done.2 = s32[4,32]{1,0:T(4,128)S(1)} collective-permute-done((s32[4,32]{1,0:T(4,128)S(1)}, s32[4,32]{1,0:T(4,128)S(1)}, u32[]{:S(2)}, u32[]{:S(2)}) %collective-permute-start.2) | collective-permute-done | bytes 544 | tf_op jit(solution)/shard_map/ppermute | solution.py:414
  121.5 6.5 %collective-permute-done.3 = s32[8,32]{1,0:T(8,128)S(1)} collective-permute-done((s32[8,32]{1,0:T(8,128)S(1)}, s32[8,32]{1,0:T(8,128)S(1)}, u32[]{:S(2)}, u32[]{:S(2)}) %collective-permute-start.3) | collective-permute-done | bytes 1056 | tf_op jit(solution)/shard_map/ppermute | solution.py:414
  128.6 2.3 collective-permute-done.4.twin_ref
  131.0 13.7 %shard_map.57 = bf16[16,128,128]{2,1,0:T(8,128)(2,1)S(1)} custom-call(s32[512]{0:T(512)S(1)} %reshape.49.labels_ref, s32[256]{0:T(256)S(1)} %reshape.50.starts_ref, s32[1]{0:T(128)} %bitcast.1.which_ref.group_ref, bf16[16,800,128]{2,1,0:T(8,128)(2,1)S(1)} %all-to-all-done.first_ref, bf16[16,400,128]{2,1,0:T(8,128)(2,1)} %collective-permute-done.4.twin_ref), custom_call_target="tpu_custom_call" | custom-call | flops 4294967296 | bytes 4915200 | tf_op jit(solution)/shard_map/pallas_call | solution.py:478
  145.4 6.8 %all-to-all-start.1 = ((bf16[16,128,128]{2,1,0:T(8,128)(2,1)}), bf16[16,128,128]{2,1,0:T(8,128)(2,1)S(1)}, u32[]{:S(2)}, u32[]{:S(2)}) async-start(bf16[16,128,128]{2,1,0:T(8,128)(2,1)} %copy-done.4), calls=%async_computation.1 | async-start | bytes 1048576 | tf_op jit(solution)/shard_map/all_to_all | solution.py:406
  152.3 1.3 collective-permute-start.5
  153.5 12.6 %all-to-all-done.1.parts_ref = bf16[16,128,128]{2,1,0:T(8,128)(2,1)S(1)} async-done(((bf16[16,128,128]{2,1,0:T(8,128)(2,1)}), bf16[16,128,128]{2,1,0:T(8,128)(2,1)S(1)}, u32[]{:S(2)}, u32[]{:S(2)}) %all-to-all-start.1) | async-done | bytes 524320 | tf_op jit(solution)/shard_map/all_to_all | solution.py:406
  166.2 18.4 %all_to_all.25.down_ref = bf16[16,128,128]{2,1,0:T(8,128)(2,1)S(1)} all-to-all(bf16[16,128,128]{2,1,0:T(8,128)(2,1)S(1)} %shard_map.58), channel_id=1, replica_groups=mesh['groups'=2,'adapter'=16] {'adapter'}, dimensions={0} | all-to-all | bytes 1048576 | tf_op jit(solution)/shard_map/all_to_all | solution.py:406
  184.6 4.9 %collective-permute-done.5.twin_ref = bf16[16,400,128]{2,1,0:T(8,128)(2,1)S(1)} collective-permute-done((bf16[16,400,128]{2,1,0:T(8,128)(2,1)}, bf16[16,400,128]{2,1,0:T(8,128)(2,1)S(1)}, u32[]{:S(2)}, u32[]{:S(2)}) %collective-permute-start.5) | collective-permute-done | bytes 1638432 | tf_op jit(solution)/shard_map/ppermute | solution.py:472
  189.5 1.2 copy-done.6
  190.7 1.4 copy-done.7
  192.1 14.0 %shard_map.59 = bf16[16,400,128]{2,1,0:T(8,128)(2,1)S(1)} custom-call(s32[512]{0:T(512)S(1)} %reshape.49.labels_ref, s32[256]{0:T(256)S(1)} %reshape.50.starts_ref, s32[1]{0:T(128)} %bitcast.1.which_ref.group_ref, bf16[16,128,128]{2,1,0:T(8,128)(2,1)S(1)} %all_to_all.25.down_ref, bf16[16,400,128]{2,1,0:T(8,128)(2,1)} %all-to-all-done.3.own_ref, ...), custom_call_target="tpu_custom_call" | custom-call | flops 4294967296 | bytes 4915200 | tf_op jit(solution)/shard_map/pallas_call | solution.py:496
  206.2 44.4 %all_to_all.26.returned_ref = bf16[16,400,128]{2,1,0:T(8,128)(2,1)S(1)} all-to-all(bf16[16,400,128]{2,1,0:T(8,128)(2,1)S(1)} %shard_map.59), channel_id=1, replica_groups=mesh['groups'=2,'adapter'=16] {'adapter'}, dimensions={0} | all-to-all | bytes 3276800 | tf_op jit(solution)/shard_map/all_to_all | solution.py:406
  250.5 2.7 %shard_map.60 = bf16[32,8,3200]{2,1,0:T(8,128)(2,1)} custom-call(s32[32]{0:T(128)S(1)} %convert_reduce_fusion.1.position_ref, s32[32]{0:T(128)S(1)} %copy-done.5, bf16[32,8,3200]{2,1,0:T(8,128)(2,1)S(1)} %copy-done.2, bf16[16,400,128]{2,1,0:T(8,128)(2,1)S(1)} %all_to_all.26.returned_ref), custom_call_target="tpu_custom_call" | custom-call | bytes 4915200 | tf_op jit(solution)/shard_map/pallas_call | solution.py:510
  (35 shorter events, 6.3 us)
Async XLA Ops:
  0.8 1.4 copy-start.1
  8.2 79.3 %all-to-all-start = ((bf16[16,800,128]{2,1,0:T(8,128)(2,1)}), bf16[16,800,128]{2,1,0:T(8,128)(2,1)S(1)}, u32[]{:S(2)}, u32[]{:S(2)}) async-start(bf16[16,800,128]{2,1,0:T(8,128)(2,1)} %shard_map.56), calls=%async_computation | async-start | bytes 6553600 | tf_op jit(solution)/shard_map/all_to_all | solution.py:406
  14.7 1.9 copy-start.3
  17.2 1.2 copy-start
  87.4 58.0 %all-to-all-start.3 = ((bf16[16,400,128]{2,1,0:T(8,128)(2,1)}), bf16[16,400,128]{2,1,0:T(8,128)(2,1)}, u32[]{:S(2)}, u32[]{:S(2)}) async-start(bf16[16,400,128]{2,1,0:T(8,128)(2,1)} %copy-done), calls=%async_computation.3 | async-start | bytes 3276800 | tf_op jit(solution)/shard_map/all_to_all | solution.py:406
  92.3 2.5 copy-start.8
  93.6 37.3 %collective-permute-start.4 = (bf16[16,400,128]{2,1,0:T(8,128)(2,1)}, bf16[16,400,128]{2,1,0:T(8,128)(2,1)}, u32[]{:S(2)}, u32[]{:S(2)}) collective-permute-start(bf16[16,400,128]{2,1,0:T(8,128)(2,1)} %slice.4), channel_id=1, source_target_pairs={{0,16},{16,0},{1,17},{17,1},{2,18},{18,2},{3,19},{19,3},{4,20},{20... | collective-permute-start | bytes 4915208 | tf_op jit(solution)/shard_map/ppermute | solution.py:461
  94.9 1.5 collective-permute-start
  96.5 3.8 %collective-permute-start.1 = (s32[2,32]{1,0:T(2,128)S(1)}, s32[2,32]{1,0:T(2,128)S(1)}, u32[]{:S(2)}, u32[]{:S(2)}) collective-permute-start(s32[2,32]{1,0:T(2,128)S(1)} %pad_add_fusion.2), channel_id=1, source_target_pairs={{0,2},{1,3},{2,0},{3,1},{4,6},{5,7},{6,4},{7,5},{8,10},{9,11},{10,... | collective-permute-start | bytes 776 | tf_op jit(solution)/shard_map/ppermute | solution.py:414
  100.3 20.0 %collective-permute-start.2 = (s32[4,32]{1,0:T(4,128)S(1)}, s32[4,32]{1,0:T(4,128)S(1)}, u32[]{:S(2)}, u32[]{:S(2)}) collective-permute-start(s32[4,32]{1,0:T(4,128)S(1)} %pad_add_fusion.1), channel_id=1, source_target_pairs={{0,4},{1,5},{2,6},{3,7},{4,0},{5,1},{6,2},{7,3},{8,12},{9,13},{10,... | collective-permute-start | bytes 1544 | tf_op jit(solution)/shard_map/ppermute | solution.py:414
  120.3 7.6 %collective-permute-start.3 = (s32[8,32]{1,0:T(8,128)S(1)}, s32[8,32]{1,0:T(8,128)S(1)}, u32[]{:S(2)}, u32[]{:S(2)}) collective-permute-start(s32[8,32]{1,0:T(8,128)S(1)} %pad_add_fusion), channel_id=1, source_target_pairs={{0,8},{1,9},{2,10},{3,11},{4,12},{5,13},{6,14},{7,15},{8,0},{9,1},... | collective-permute-start | bytes 3080 | tf_op jit(solution)/shard_map/ppermute | solution.py:414
  144.6 0.8 copy-start.4
  145.4 20.7 %all-to-all-start.1 = ((bf16[16,128,128]{2,1,0:T(8,128)(2,1)}), bf16[16,128,128]{2,1,0:T(8,128)(2,1)S(1)}, u32[]{:S(2)}, u32[]{:S(2)}) async-start(bf16[16,128,128]{2,1,0:T(8,128)(2,1)} %copy-done.4), calls=%async_computation.1 | async-start | bytes 1048576 | tf_op jit(solution)/shard_map/all_to_all | solution.py:406
  152.3 37.2 %collective-permute-start.5 = (bf16[16,400,128]{2,1,0:T(8,128)(2,1)}, bf16[16,400,128]{2,1,0:T(8,128)(2,1)S(1)}, u32[]{:S(2)}, u32[]{:S(2)}) collective-permute-start(bf16[16,400,128]{2,1,0:T(8,128)(2,1)} %all-to-all-done.3.own_ref), channel_id=1, source_target_pairs={{0,16},{16,0},{1,17},{17,1},{2,18},{18,2},{3,19},{19,3},{4,20},{20... | collective-permute-start | bytes 4915208 | tf_op jit(solution)/shard_map/ppermute | solution.py:472
  189.5 1.2 copy-start.6
  190.7 1.4 copy-start.7
  206.1 44.4 %copy-start.2 = (bf16[32,8,3200]{2,1,0:T(8,128)(2,1)S(1)}, bf16[32,8,3200]{2,1,0:T(8,128)(2,1)}, u32[]{:S(2)}) copy-start(bf16[32,8,3200]{2,1,0:T(8,128)(2,1)} %tokens_ref.3) | copy-start | bytes 4915204
  206.2 44.4 %copy-start.5 = (s32[32]{0:T(128)S(1)}, s32[32]{0:T(128)}, u32[]{:S(2)}) copy-start(s32[32]{0:T(128)} %used_ref.1) | copy-start | bytes 388
